TPU v7x, 512 devices: a whole 4x8x8 slice. The times are simulated.
512 devices in a mesh: hours: 64 (over z, x, core), region: 8 (over y).
Axes of the slice: x: 4, y: 8, z: 8, core: 2. Of those that a mesh axis runs over, the one named last changes fastest.
Arguments:
- availability: float32 [4096, 16, 1024], P('hours', None, 'region'), may hold values from 0.1 to 1
- demand: float32 [4096, 1024], P('hours', 'region'), may hold values from 2 to 72, as said below
- gen_cost: float32 [16, 1024], P(None, 'region'), may hold values from 0.05 to 1
- cap_cost: float32 [8, 2048], P('region', 'hours'), may hold values from 204.8 to 2048
- owner_map: int32 [8, 2048], P('region'), may hold values from 0 to 2047, each once within a row
- line_ends: int32 [2, 2048], P(None, 'region'), may hold values from 0 to 127
- line_limit: float32 [2048], P('region'), may hold values from 0.5 to 4
- cross_ends: int32 [2, 8, 256], P(None, 'region'), may hold values from 0 to 127
- cross_limit: float32 [8, 256], P('region'), may hold values from 0.5 to 4
- pair_counts: int32 [8, 8], P('region'), may hold values from 0 to 32, as said below
- store_node: int32 [2048], P('region'), may hold values from 0 to 127
- store_energy: float32 [2048], P('region'), may hold values from 0.02 to 0.4
- store_power: float32 [2048], P('region'), may hold values from 0.2 to 2
- price_start: float32 [4096, 1024], P('hours', 'region'), may hold values from -3 to 0.5
Outputs:
- dispatch: float32 [4096, 16, 1024], P('hours', None, 'region')
- capacity: float32 [8, 2048], P('region', 'hours')
- prices: float32 [4096, 1024], P('hours', 'region')
- charge_state: float32 [4096, 2048], P('hours', 'region')
Inputs may be any that keep to these rules, and one draw needn't show every extreme that they name: `demand`: loads are positive. `owner_map`: each row lists every capacity column of its region once. `pair_counts`: cross lines in use among the 32 slots of each ordered pair of regions; a region has none to itself; some pair uses all 32.
All inputs are finite; a program needn't handle non-finite values.
Results may differ from a plain program's by a relative error of at most 0.00018.
Values sent between devices are 32-bit elements; how exact they have to be, the bound alone decides.
A program may use at most 64 MiB of HBM per device.

v0:
```python
import jax
import jax.numpy as jnp
from jax import lax
from jax.sharding import PartitionSpec as P

ITERS = 4
epsilon = 1e-06
highest = lax.Precision.HIGHEST


def shifted(value, axis, steps):
    count = lax.axis_size(axis)
    pairs = [(source, (source + steps) % count) for source in range(count)]
    return lax.ppermute(value, axis, pairs)


def one_hot(indices, labels):
    return (indices[:, None] == labels[None, :]).astype(jnp.float32)


def to_owners(partial_value, owned_cols):
    summed = lax.psum(partial_value, "hours")
    return lax.dynamic_slice_in_dim(summed, lax.axis_index("hours") * owned_cols, owned_cols)


def spread_columns(capacity_bar):
    return lax.all_gather(capacity_bar, "hours", axis=0, tiled=True)


def body(
    availability,
    demand,
    gen_cost,
    cap_cost,
    owner_map,
    line_ends,
    line_limit,
    cross_ends,
    cross_limit,
    pair_counts,
    store_node,
    store_energy,
    store_power,
    price_start,
):
    hour_rows, tech_count, node_count = availability.shape
    region_count = lax.axis_size("region")
    slot_count = cross_limit.shape[1]
    slot_width = slot_count // region_count
    owned_cols = cap_cost.shape[1]
    owner_cols = owner_map[0]
    inverse = jnp.argsort(owner_cols)
    node_ids = jnp.arange(node_count, dtype=jnp.int32)
    line_inc = one_hot(line_ends[1], node_ids) - one_hot(line_ends[0], node_ids)
    store_map = one_hot(store_node, node_ids)
    leave_map = one_hot(cross_ends[0, 0], node_ids)
    slot_ids = jnp.arange(slot_count, dtype=jnp.int32)
    pair_of = slot_ids // slot_width
    region_ids = jnp.arange(region_count, dtype=jnp.int32)
    in_use = jnp.sum(
        jnp.where(pair_of[:, None] == region_ids[None, :], pair_counts[0][None, :], 0), axis=1
    )
    cross_bound = jnp.where(slot_ids % slot_width < in_use, cross_limit[0], 0.0)
    reach_map = one_hot(
        pair_of * node_count + cross_ends[1, 0],
        jnp.arange(region_count * node_count, dtype=jnp.int32),
    )
    column_costs = cap_cost[0]
    col_weight = to_owners(jnp.sum(availability, axis=0).reshape(-1)[owner_cols], owned_cols)
    dispatch = jnp.zeros_like(availability)
    capacity = jnp.zeros((owned_cols,), jnp.float32)
    inner_flow = jnp.zeros((hour_rows, line_limit.shape[0]), jnp.float32)
    cross_flow = jnp.zeros((hour_rows, slot_count), jnp.float32)
    mirror_flow = jnp.zeros((hour_rows, slot_count), jnp.float32)
    discharge = jnp.zeros((hour_rows, store_node.shape[0]), jnp.float32)
    charge = jnp.zeros((hour_rows, store_node.shape[0]), jnp.float32)
    prices = price_start
    cap_duals = jnp.zeros_like(availability)
    store_duals = jnp.zeros((hour_rows, store_node.shape[0]), jnp.float32)
    weight = jnp.float32(1.0)
    for iteration in range(ITERS):
        final_sweep = iteration == ITERS - 1
        primal_step = 0.5 / weight
        far_side = jnp.dot(
            lax.all_gather(prices, "region", axis=1, tiled=True), reach_map.T, precision=highest
        )
        if iteration == 0:
            next_duals = jnp.zeros_like(store_duals)
            cap_pull = jnp.zeros((owned_cols,), jnp.float32)
        else:
            next_row = shifted(store_duals[:1], "hours", -1)
            next_duals = jnp.concatenate([store_duals[1:], next_row], axis=0)
            cap_pull = to_owners(
                jnp.sum(availability * cap_duals, axis=0).reshape(-1)[owner_cols], owned_cols
            )
        dispatch_new = jnp.maximum(
            dispatch - primal_step * (gen_cost[None] + prices[:, None, :] + cap_duals), 0.0
        )
        capacity_new = jnp.maximum(
            capacity - (column_costs - cap_pull) / (weight * col_weight), 0.0
        )
        inner_new = jnp.clip(
            inner_flow - primal_step * jnp.dot(prices, line_inc.T, precision=highest),
            -line_limit,
            line_limit,
        )
        cross_new = jnp.clip(
            cross_flow - primal_step * (far_side - jnp.dot(prices, leave_map.T, precision=highest)),
            -cross_bound,
            cross_bound,
        )
        mirror_new = mirror_flow
        discharge_new = jnp.clip(
            discharge
            - primal_step * (jnp.dot(prices, store_map.T, precision=highest) + store_duals),
            -store_power,
            store_power,
        )
        charge_new = jnp.clip(charge - primal_step * (store_duals - next_duals), 0.0, store_energy)
        if not final_sweep:
            cap_change = capacity_new - capacity
            primal_sq = (
                jnp.sum((dispatch_new - dispatch) ** 2)
                + jnp.sum(cap_change**2)
                + jnp.sum((inner_new - inner_flow) ** 2)
                + jnp.sum((cross_new - cross_flow) ** 2)
                + jnp.sum((discharge_new - discharge) ** 2)
                + jnp.sum((charge_new - charge) ** 2)
            )
            primal_sum = lax.psum(primal_sq, ("hours", "region"))
        dispatch_bar = 2.0 * dispatch_new - dispatch
        capacity_bar = 2.0 * capacity_new - capacity
        inner_bar = 2.0 * inner_new - inner_flow
        cross_bar = 2.0 * cross_new - cross_flow
        discharge_bar = 2.0 * discharge_new - discharge
        charge_bar = 2.0 * charge_new - charge
        capacity_all = spread_columns(capacity_bar)
        cap_dense = capacity_all[inverse].reshape(tech_count, node_count)
        per_dest = jnp.dot(cross_bar, reach_map, precision=highest)
        balance = (
            jnp.sum(dispatch_bar, axis=1)
            + jnp.dot(inner_bar, line_inc, precision=highest)
            + (
                lax.psum_scatter(per_dest, "region", scatter_dimension=1, tiled=True)
                - jnp.dot(cross_bar, leave_map, precision=highest)
            )
            + jnp.dot(discharge_bar, store_map, precision=highest)
            - demand
        )
        prev_row = shifted(charge_bar[-1:], "hours", 1)
        storage_rows = (
            charge_bar - jnp.concatenate([prev_row, charge_bar[:-1]], axis=0) + discharge_bar
        )
        cap_rows = dispatch_bar - availability * cap_dense[None]
        prices_new = prices + weight / (tech_count + 8.0) * balance
        cap_new = jnp.maximum(cap_duals + weight / 2.0 * cap_rows, 0.0)
        store_new = store_duals + weight / 3.0 * storage_rows
        if not final_sweep:
            dual_sq = (
                jnp.sum((prices_new - prices) ** 2)
                + jnp.sum((cap_new - cap_duals) ** 2)
                + jnp.sum((store_new - store_duals) ** 2)
            )
            dual_sum = lax.psum(dual_sq, ("hours", "region"))
            weight = jnp.sqrt(weight * jnp.sqrt((dual_sum + epsilon) / (primal_sum + epsilon)))
        dispatch, capacity, inner_flow, cross_flow = (
            dispatch_new,
            capacity_new,
            inner_new,
            cross_new,
        )
        mirror_flow = mirror_new
        discharge, charge = (discharge_new, charge_new)
        prices, cap_duals, store_duals = (prices_new, cap_new, store_new)
    return (dispatch, capacity[None], prices, charge)


def solution(mesh):
    placed = (
        P("hours", None, "region"),
        P("hours", "region"),
        P(None, "region"),
        P("region", "hours"),
        P("region", None),
        P(None, "region"),
        P("region"),
        P(None, "region", None),
        P("region", None),
        P("region", None),
        P("region"),
        P("region"),
        P("region"),
        P("hours", "region"),
    )
    return jax.shard_map(
        body,
        mesh=mesh,
        in_specs=placed,
        out_specs=(
            P("hours", None, "region"),
            P("region", "hours"),
            P("hours", "region"),
            P("hours", "region"),
        ),
        check_vma=False,
    )
```

profile of v0, /device:TPU:2, one launch (start us, length us, event | category | flops | bytes accessed | tf_op | source)
XLA Modules:
  0.0 1496.5 jit_solution(16780039333863139814)
XLA Ops:
  7.2 0.7 broadcast_minimum_fusion
  7.9 2.0 collective-permute-start
  10.0 26.6 %all_gather.21 = f32[64,1024]{1,0:T(8,128)S(1)} all-gather(f32[64,128]{1,0:T(8,128)} %param.27), channel_id=1, replica_groups=mesh['hours'=64,'region'=8] {'region'}, dimensions={1}, use_global_device_ids=true | all-gather | bytes 294912 | tf_op jit(solution)/shard_map/all_gather | solution.py:85
  37.3 0.7 fusion.75
  38.1 0.9 multiply_reduce_fusion.20
  39.0 1.3 fusion.74
  41.2 11.8 gather_fusion
  53.0 126.8 %psum.70 = f32[2048]{0:T(1024)S(1)} all-reduce(f32[2048]{0:T(1024)S(1)} %gather_fusion), channel_id=1, replica_groups=mesh['hours'=64,'region'=8] {'hours'}, use_global_device_ids=true, to_apply=%region_5.6 | all-reduce | flops 2048 | bytes 16384 | tf_op jit(solution)/shard_map/psum | solution.py:22
  179.7 1.3 dynamic-slice
  181.7 0.7 multiply_reduce_fusion.28
  182.5 126.4 %all-reduce = f32[2048]{0:T(1024)S(1)} all-reduce(f32[2048]{0:T(1024)S(1)} %multiply_dynamic-update-slice_fusion), channel_id=1, replica_groups=mesh['hours'=64,'region'=8] {'hours'}, use_global_device_ids=true, to_apply=%add | all-reduce | flops 2048 | bytes 16384
  308.9 5.0 sort.17
  314.0 11.8 gather_fusion.1
  325.8 1.1 multiply_reduce_fusion.6
  326.8 11.8 gather_fusion.2
  338.6 1.0 multiply_reduce_fusion.21
  339.6 0.7 broadcast_reduce_fusion
  340.6 126.1 %psum.73 = f32[2048]{0:T(1024)S(1)} all-reduce(f32[2048]{0:T(1024)S(1)} %gather_fusion.2), channel_id=1, replica_groups=mesh['hours'=64,'region'=8] {'hours'}, use_global_device_ids=true, to_apply=%region_21.22 | all-reduce | flops 2048 | bytes 16384 | tf_op jit(solution)/shard_map/psum | solution.py:22
  469.9 0.9 multiply_reduce_fusion.19
  472.2 1.0 fusion.67
  473.2 0.9 multiply_reduce_fusion.25
  476.0 7.0 collective-permute-start.1
  483.0 95.3 %all-reduce.5 = (f32[]{:T(128)}, f32[]{:T(128)}) all-reduce(f32[]{:T(128)S(6)} %add.309, f32[]{:T(128)S(6)} %add.315), channel_id=1, replica_groups=mesh['hours'=64,'region'=8] {'hours','region'}, use_global_device_ids=true, to_apply=%region_9.10 | all-reduce | flops 2 | bytes 16 | tf_op jit(solution)/shard_map/psum | solution.py:164
  579.7 24.8 %all_gather.23 = f32[64,1024]{1,0:T(8,128)S(1)} all-gather(f32[64,128]{1,0:T(8,128)S(1)} %get-tuple-element.56), channel_id=1, replica_groups=mesh['hours'=64,'region'=8] {'region'}, dimensions={1}, use_global_device_ids=true | all-gather | bytes 294912 | tf_op jit(solution)/shard_map/all_gather | solution.py:85
  604.5 1.0 multiply_reduce_fusion.17
  605.6 0.7 multiply_reduce_fusion.27
  606.4 120.4 %all-reduce.1 = f32[2048]{0:T(1024)S(1)} all-reduce(f32[2048]{0:T(1024)S(1)} %subtract_dynamic-update-slice_fusion.1), channel_id=1, replica_groups=mesh['hours'=64,'region'=8] {'hours'}, use_global_device_ids=true, to_apply=%add.1 | all-reduce | flops 2048 | bytes 16384
  726.8 11.8 gather_fusion.3
  739.9 0.7 fusion.73
  740.7 0.9 multiply_reduce_fusion.16
  741.6 1.3 fusion.72
  742.9 1.2 multiply_reduce_fusion.3
  744.2 11.8 gather_fusion.4
  756.0 1.9 collective-permute-start.2
  758.2 131.1 %psum.76 = f32[2048]{0:T(1024)S(1)} all-reduce(f32[2048]{0:T(1024)S(1)} %gather_fusion.4), channel_id=1, replica_groups=mesh['hours'=64,'region'=8] {'hours'}, use_global_device_ids=true, to_apply=%region_36.37 | all-reduce | flops 2048 | bytes 16384 | tf_op jit(solution)/shard_map/psum | solution.py:22
  891.9 1.0 multiply_reduce_fusion.15
  894.2 1.0 fusion.63
  895.2 0.9 multiply_reduce_fusion.24
  898.0 1.9 collective-permute-start.3
  900.0 100.8 %all-reduce.4 = (f32[]{:T(128)}, f32[]{:T(128)}) all-reduce(f32[]{:T(128)S(6)} %add.329, f32[]{:T(128)S(6)} %add.335), channel_id=1, replica_groups=mesh['hours'=64,'region'=8] {'hours','region'}, use_global_device_ids=true, to_apply=%region_24.25 | all-reduce | flops 2 | bytes 16 | tf_op jit(solution)/shard_map/psum | solution.py:164
  1002.2 0.7 multiply_reduce_fusion.26
  1002.9 1.0 multiply_reduce_fusion.12
  1003.9 24.8 %all_gather.25 = f32[64,1024]{1,0:T(8,128)S(1)} all-gather(f32[64,128]{1,0:T(8,128)S(1)} %get-tuple-element.63), channel_id=1, replica_groups=mesh['hours'=64,'region'=8] {'region'}, dimensions={1}, use_global_device_ids=true | all-gather | bytes 294912 | tf_op jit(solution)/shard_map/all_gather | solution.py:85
  1029.5 120.4 %all-reduce.2 = f32[2048]{0:T(1024)S(1)} all-reduce(f32[2048]{0:T(1024)S(1)} %subtract_dynamic-update-slice_fusion), channel_id=1, replica_groups=mesh['hours'=64,'region'=8] {'hours'}, use_global_device_ids=true, to_apply=%add.2 | all-reduce | flops 2048 | bytes 16384
  1149.9 11.8 gather_fusion.5
  1161.7 1.9 collective-permute-start.4
  1163.7 0.7 fusion.71
  1164.4 0.9 multiply_reduce_fusion.11
  1165.3 1.3 fusion.70
  1166.7 1.4 multiply_reduce_fusion
  1168.1 11.8 gather_fusion.6
  1180.2 131.1 %psum.79 = f32[2048]{0:T(1024)S(1)} all-reduce(f32[2048]{0:T(1024)S(1)} %gather_fusion.6), channel_id=1, replica_groups=mesh['hours'=64,'region'=8] {'hours'}, use_global_device_ids=true, to_apply=%region_48.49 | all-reduce | flops 2048 | bytes 16384 | tf_op jit(solution)/shard_map/psum | solution.py:22
  1313.9 0.9 multiply_reduce_fusion.13
  1316.2 1.0 fusion.59
  1317.2 0.9 multiply_reduce_fusion.23
  1320.0 1.9 collective-permute-start.5
  1321.9 100.9 %all-reduce.3 = (f32[]{:T(128)}, f32[]{:T(128)}) all-reduce(f32[]{:T(128)S(6)} %add.349, f32[]{:T(128)S(6)} %add.355), channel_id=1, replica_groups=mesh['hours'=64,'region'=8] {'hours','region'}, use_global_device_ids=true, to_apply=%region_39.40 | all-reduce | flops 2 | bytes 16 | tf_op jit(solution)/shard_map/psum | solution.py:164
  1424.3 24.8 %all_gather.27 = f32[64,1024]{1,0:T(8,128)S(1)} all-gather(f32[64,128]{1,0:T(8,128)S(1)} %get-tuple-element.70), channel_id=1, replica_groups=mesh['hours'=64,'region'=8] {'region'}, dimensions={1}, use_global_device_ids=true | all-gather | bytes 294912 | tf_op jit(solution)/shard_map/all_gather | solution.py:85
  1449.5 1.6 subtract_reduce_fusion
  1451.0 0.7 fusion.69
  1452.1 1.3 fusion.68
  1455.2 32.9 %reduce-scatter.11.cloned.1.call-done = f32[64,128]{1,0:T(8,128)} async-done(((f32[64,1024]{1,0:T(8,128)}), f32[64,128]{1,0:T(8,128)}) %reduce-scatter.11.cloned.1.call-update) | async-done | bytes 32784 | tf_op jit(solution)/shard_map/reduce_scatter | solution.py:144
  1488.1 1.0 fusion.55
  1489.1 0.9 fusion.54
  (86 shorter events, 8.4 us)
Async XLA Ops:
  7.2 465.0 %reduce-scatter.5.cloned.1.call-start = ((), (), s32[]{:S(2)}) async-start(), calls=%async_computation.4 | async-start | bytes 294912 | tf_op jit(solution)/shard_map/reduce_scatter | solution.py:144
  7.9 2.1 copy-start.9
  7.9 461.4 %collective-permute-start = (f32[1,256]{1,0:T(1,128)S(1)}, f32[1,256]{1,0:T(1,128)S(1)}, u32[]{:S(2)}, u32[]{:S(2)}) collective-permute-start(f32[1,256]{1,0:T(1,128)S(1)} %bitcast.122), channel_id=1, source_target_pairs={{0,8},{8,16},{16,24},{24,32},{32,40},{40,48},{48,56},{56,64},{64,7... | collective-permute-start | bytes 3080 | tf_op jit(solution)/shard_map/ppermute | solution.py:14
  36.6 0.7 copy-start.13
  36.6 0.7 copy-start.12
  37.2 0.8 copy-start.1
  37.3 3.8 copy-start
  40.3 853.9 %reduce-scatter.7.cloned.1.call-start = ((), (), s32[]{:S(2)}) async-start(), calls=%async_computation.5 | async-start | bytes 294912 | tf_op jit(solution)/shard_map/reduce_scatter | solution.py:144
  40.3 0.7 copy-start.11
  40.3 0.7 copy-start.5
  40.4 0.7 copy-start.10
  181.0 0.7 copy-start.8
  314.0 11.8 copy-start.3
  340.6 126.1 %copy-start.7 = (f32[256]{0:T(256)S(1)}, f32[256]{0:T(256)}, u32[]{:S(2)}) copy-start(f32[256]{0:T(256)} %param.26) | copy-start | bytes 3076
  469.2 0.7 copy-start.4
  472.1 1.1 copy-start.2
  476.0 262.6 %collective-permute-start.1 = (f32[1,256]{1,0:T(1,128)S(1)}, f32[1,256]{1,0:T(1,128)S(1)}, u32[]{:S(2)}, u32[]{:S(2)}) collective-permute-start(f32[1,256]{1,0:T(1,128)S(1)} %slice.79), channel_id=1, source_target_pairs={{0,504},{8,0},{16,8},{24,16},{32,24},{40,32},{48,40},{56,48},{64,5... | collective-permute-start | bytes 3080 | tf_op jit(solution)/shard_map/ppermute | solution.py:14
  738.6 0.7 copy-start.6
  742.9 573.2 %reduce-scatter.9.cloned.1.call-start = ((), (), s32[]{:S(2)}) async-start(), calls=%async_computation.6 | async-start | bytes 294912 | tf_op jit(solution)/shard_map/reduce_scatter | solution.py:144
  756.0 135.9 %collective-permute-start.2 = (f32[1,256]{1,0:T(1,128)S(1)}, f32[1,256]{1,0:T(1,128)S(1)}, u32[]{:S(2)}, u32[]{:S(2)}) collective-permute-start(f32[1,256]{1,0:T(1,128)S(1)} %slice.80), channel_id=1, source_target_pairs={{0,8},{8,16},{16,24},{24,32},{32,40},{40,48},{48,56},{56,64},{64,7... | collective-permute-start | bytes 3080 | tf_op jit(solution)/shard_map/ppermute | solution.py:14
  898.0 130.7 %collective-permute-start.3 = (f32[1,256]{1,0:T(1,128)S(1)}, f32[1,256]{1,0:T(1,128)S(1)}, u32[]{:S(2)}, u32[]{:S(2)}) collective-permute-start(f32[1,256]{1,0:T(1,128)S(1)} %slice.83), channel_id=1, source_target_pairs={{0,504},{8,0},{16,8},{24,16},{32,24},{40,32},{48,40},{56,48},{64,5... | collective-permute-start | bytes 3080 | tf_op jit(solution)/shard_map/ppermute | solution.py:14
  1161.7 152.2 %collective-permute-start.4 = (f32[1,256]{1,0:T(1,128)S(1)}, f32[1,256]{1,0:T(1,128)S(1)}, u32[]{:S(2)}, u32[]{:S(2)}) collective-permute-start(f32[1,256]{1,0:T(1,128)S(1)} %slice.84), channel_id=1, source_target_pairs={{0,8},{8,16},{16,24},{24,32},{32,40},{40,48},{48,56},{56,64},{64,7... | collective-permute-start | bytes 3080 | tf_op jit(solution)/shard_map/ppermute | solution.py:14
  1166.6 321.5 %reduce-scatter.11.cloned.1.call-start = ((), (), s32[]{:S(2)}) async-start(), calls=%async_computation.7 | async-start | bytes 294912 | tf_op jit(solution)/shard_map/reduce_scatter | solution.py:144
  1320.0 134.3 %collective-permute-start.5 = (f32[1,256]{1,0:T(1,128)S(1)}, f32[1,256]{1,0:T(1,128)S(1)}, u32[]{:S(2)}, u32[]{:S(2)}) collective-permute-start(f32[1,256]{1,0:T(1,128)S(1)} %slice.87), channel_id=1, source_target_pairs={{0,504},{8,0},{16,8},{24,16},{32,24},{40,32},{48,40},{56,48},{64,5... | collective-permute-start | bytes 3080 | tf_op jit(solution)/shard_map/ppermute | solution.py:14
Sparse Core Ops, SparseCore 0:
  40.4 42.1 reduce-scatter.4
  743.0 39.1 reduce-scatter.6
  1166.7 41.5 reduce-scatter.8
  1453.5 34.5 reduce-scatter.10
where the time goes:
time: 1500 us
  blocking collectives  1280 us (85%)
  local copies, waits for them, and re-layouts  86.5 us (6%)
  between operations  36.6 us (2%)
  waiting for transfers between devices  33 us (2%)
  matrix products  26.5 us (2%)
  starting transfers between devices  16.8 us (1%)
  other arithmetic  16.8 us (1%)
    psum x4, blocking collectives, to_owners(): summed = lax.psum(partial_value, 'hours')  515 us
    unnamed x3, blocking collectives  367 us
    psum x3, blocking collectives, body(): dual_sum = lax.psum(dual_sq, ('hours', 'region'))  297 us
    all_gather x4, blocking collectives, body(): lax.all_gather(prices, 'region', axis=1, tiled=True)  101 us
    gather x3, local copies, waits for them, and re-layouts, body(): cap_dense = capacity_all[inverse].reshape(tech_count, node_count)  35.3 us
    gather x3, local copies, waits for them, and re-layouts, body(): jnp.sum(availability * cap_duals, axis=0).reshape(-1)[owner_cols]  35.3 us
    reduce_scatter x4, waiting for transfers between devices, body(): lax.psum_scatter(per_dest, 'region', scatter_dimension=1, tiled=True)  32.9 us
  transfers between devices with their start and end apart: 10, of which 1 were waited for; matrix products, arithmetic and copies ran while one was open for 7% of the time, Pallas kernels for 0%

commit v1 on v0

--- a/solution.py
+++ b/solution.py
@@ -82,7 +82,12 @@
         final_sweep = iteration == ITERS - 1
         primal_step = 0.5 / weight
         far_side = jnp.dot(
-            lax.all_gather(prices, "region", axis=1, tiled=True), reach_map.T, precision=highest
+            jnp.concatenate(
+                lax.all_to_all(jnp.stack([prices] * lax.axis_size("region")), "region", 0, 0),
+                axis=1,
+            ),
+            reach_map.T,
+            precision=highest,
         )
         if iteration == 0:
             next_duals = jnp.zeros_like(store_duals)

time: 1500 us -> 1440 us (0.960)
  blocking collectives: 1280 us -> 1190 us
  starting transfers between devices: 16.8 us -> 40.2 us
    all_gather x4 -> x0, blocking collectives: 101 us -> none  [body(): lax.all_gather(prices, 'region', axis=1, tiled=True)]
    all_to_all x0 -> x4, starting transfers between devices: none -> 23.4 us  [body(): lax.all_to_all(jnp.stack([prices] * lax.axis_size('region')), 'region', 0...]
  transfers between devices with their start and end apart: 10 -> 14, of which waited for: 1 -> 2; matrix products, arithmetic and copies ran while one was open for 7% -> 8% of each run, Pallas kernels for 0% -> 0%
where the time goes in v1:
time: 1440 us
  blocking collectives  1190 us (83%)
  local copies, waits for them, and re-layouts  91.4 us (6%)
  starting transfers between devices  40.2 us (3%)
  waiting for transfers between devices  39.6 us (3%)
  between operations  36.6 us (3%)
  matrix products  26.5 us (2%)
  other arithmetic  16.7 us (1%)
    psum x4, blocking collectives, to_owners(): summed = lax.psum(partial_value, 'hours')  520 us
    unnamed x3, blocking collectives  371 us
    psum x3, blocking collectives, body(): dual_sum = lax.psum(dual_sq, ('hours', 'region'))  300 us
    gather x3, local copies, waits for them, and re-layouts, body(): cap_dense = capacity_all[inverse].reshape(tech_count, node_count)  35.3 us
    gather x3, local copies, waits for them, and re-layouts, body(): jnp.sum(availability * cap_duals, axis=0).reshape(-1)[owner_cols]  35.3 us
    reduce_scatter x4, waiting for transfers between devices, body(): lax.psum_scatter(per_dest, 'region', scatter_dimension=1, tiled=True)  29.9 us
  transfers between devices with their start and end apart: 14, of which 2 were waited for; matrix products, arithmetic and copies ran while one was open for 8% of the time, Pallas kernels for 0%

profile of v1, /device:TPU:2, one launch (start us, length us, event | category | flops | bytes accessed | tf_op | source)
XLA Modules:
  0.0 1442.1 jit_solution(13125214593106681847)
XLA Ops:
  7.2 0.7 broadcast_minimum_fusion
  7.9 1.9 collective-permute-start
  9.8 1.5 stack.8
  11.3 7.1 all-to-all-start
  19.3 11.8 gather_fusion
  31.1 131.4 %psum.70 = f32[2048]{0:T(1024)S(1)} all-reduce(f32[2048]{0:T(1024)S(1)} %gather_fusion), channel_id=1, replica_groups=mesh['hours'=64,'region'=8] {'hours'}, use_global_device_ids=true, to_apply=%region_5.6 | all-reduce | flops 2048 | bytes 16384 | tf_op jit(solution)/shard_map/psum | solution.py:22
  162.5 1.3 dynamic-slice
  165.3 126.1 %all-reduce = f32[2048]{0:T(1024)S(1)} all-reduce(f32[2048]{0:T(1024)S(1)} %multiply_dynamic-update-slice_fusion), channel_id=1, replica_groups=mesh['hours'=64,'region'=8] {'hours'}, use_global_device_ids=true, to_apply=%add | all-reduce | flops 2048 | bytes 16384
  291.4 5.0 sort.17
  296.4 11.8 gather_fusion.1
  308.2 1.1 multiply_reduce_fusion.6
  310.6 11.8 gather_fusion.2
  323.1 1.0 multiply_reduce_fusion.21
  324.1 0.7 fusion.75
  324.8 0.9 multiply_reduce_fusion.20
  325.8 1.3 fusion.74
  328.0 126.1 %psum.73 = f32[2048]{0:T(1024)S(1)} all-reduce(f32[2048]{0:T(1024)S(1)} %gather_fusion.2), channel_id=1, replica_groups=mesh['hours'=64,'region'=8] {'hours'}, use_global_device_ids=true, to_apply=%region_21.22 | all-reduce | flops 2048 | bytes 16384 | tf_op jit(solution)/shard_map/psum | solution.py:22
  456.7 1.0 multiply_reduce_fusion.19
  459.6 1.0 fusion.67
  460.7 0.9 multiply_reduce_fusion.25
  463.5 7.0 collective-permute-start.1
  470.4 96.9 %all-reduce.5 = (f32[]{:T(128)}, f32[]{:T(128)}) all-reduce(f32[]{:T(128)S(6)} %add.309, f32[]{:T(128)S(6)} %add.315), channel_id=1, replica_groups=mesh['hours'=64,'region'=8] {'hours','region'}, use_global_device_ids=true, to_apply=%region_9.10 | all-reduce | flops 2 | bytes 16 | tf_op jit(solution)/shard_map/psum | solution.py:169
  568.7 0.7 stack.9
  569.4 5.4 all-to-all-start.1
  577.1 122.4 %all-reduce.1 = f32[2048]{0:T(1024)S(1)} all-reduce(f32[2048]{0:T(1024)S(1)} %subtract_dynamic-update-slice_fusion.1), channel_id=1, replica_groups=mesh['hours'=64,'region'=8] {'hours'}, use_global_device_ids=true, to_apply=%add.1 | all-reduce | flops 2048 | bytes 16384
  699.5 11.8 gather_fusion.3
  711.3 1.0 multiply_reduce_fusion.17
  712.3 0.7 fusion.73
  713.0 1.0 multiply_reduce_fusion.16
  714.0 1.3 fusion.72
  715.3 1.2 multiply_reduce_fusion.3
  716.5 11.8 gather_fusion.4
  728.3 1.9 collective-permute-start.2
  730.5 131.1 %psum.76 = f32[2048]{0:T(1024)S(1)} all-reduce(f32[2048]{0:T(1024)S(1)} %gather_fusion.4), channel_id=1, replica_groups=mesh['hours'=64,'region'=8] {'hours'}, use_global_device_ids=true, to_apply=%region_36.37 | all-reduce | flops 2048 | bytes 16384 | tf_op jit(solution)/shard_map/psum | solution.py:22
  863.6 1.0 multiply_reduce_fusion.15
  866.5 1.0 fusion.63
  867.5 0.9 multiply_reduce_fusion.24
  870.3 1.9 collective-permute-start.3
  872.2 101.9 %all-reduce.4 = (f32[]{:T(128)}, f32[]{:T(128)}) all-reduce(f32[]{:T(128)S(6)} %add.329, f32[]{:T(128)S(6)} %add.335), channel_id=1, replica_groups=mesh['hours'=64,'region'=8] {'hours','region'}, use_global_device_ids=true, to_apply=%region_24.25 | all-reduce | flops 2 | bytes 16 | tf_op jit(solution)/shard_map/psum | solution.py:169
  975.5 0.7 stack.10
  976.3 5.4 all-to-all-start.2
  983.4 122.4 %all-reduce.2 = f32[2048]{0:T(1024)S(1)} all-reduce(f32[2048]{0:T(1024)S(1)} %subtract_dynamic-update-slice_fusion), channel_id=1, replica_groups=mesh['hours'=64,'region'=8] {'hours'}, use_global_device_ids=true, to_apply=%add.2 | all-reduce | flops 2048 | bytes 16384
  1105.8 11.8 gather_fusion.5
  1117.6 1.9 collective-permute-start.4
  1119.5 1.0 multiply_reduce_fusion.12
  1120.6 0.7 fusion.71
  1121.3 0.9 multiply_reduce_fusion.11
  1122.2 1.3 fusion.70
  1123.5 1.4 multiply_reduce_fusion
  1124.9 11.8 gather_fusion.6
  1137.1 131.1 %psum.79 = f32[2048]{0:T(1024)S(1)} all-reduce(f32[2048]{0:T(1024)S(1)} %gather_fusion.6), channel_id=1, replica_groups=mesh['hours'=64,'region'=8] {'hours'}, use_global_device_ids=true, to_apply=%region_48.49 | all-reduce | flops 2048 | bytes 16384 | tf_op jit(solution)/shard_map/psum | solution.py:22
  1270.2 0.9 multiply_reduce_fusion.13
  1273.0 1.0 fusion.59
  1274.0 0.9 multiply_reduce_fusion.23
  1276.8 1.9 collective-permute-start.5
  1278.8 101.7 %all-reduce.3 = (f32[]{:T(128)}, f32[]{:T(128)}) all-reduce(f32[]{:T(128)S(6)} %add.349, f32[]{:T(128)S(6)} %add.355), channel_id=1, replica_groups=mesh['hours'=64,'region'=8] {'hours','region'}, use_global_device_ids=true, to_apply=%region_39.40 | all-reduce | flops 2 | bytes 16 | tf_op jit(solution)/shard_map/psum | solution.py:169
  1382.7 5.4 all-to-all-start.3
  1388.1 1.6 subtract_reduce_fusion
  1390.4 9.6 all-to-all-done.3
  1400.0 0.7 fusion.69
  1401.0 1.3 fusion.68
  1403.8 29.9 %reduce-scatter.11.cloned.1.call-done = f32[64,128]{1,0:T(8,128)} async-done(((f32[64,1024]{1,0:T(8,128)}), f32[64,128]{1,0:T(8,128)}) %reduce-scatter.11.cloned.1.call-update) | async-done | bytes 32784 | tf_op jit(solution)/shard_map/reduce_scatter | solution.py:149
  1433.7 1.0 fusion.55
  1434.7 0.9 fusion.54
  (94 shorter events, 13.2 us)
Async XLA Ops:
  7.2 12.1 copy-start
  7.9 448.1 %collective-permute-start = (f32[1,256]{1,0:T(1,128)S(1)}, f32[1,256]{1,0:T(1,128)S(1)}, u32[]{:S(2)}, u32[]{:S(2)}) collective-permute-start(f32[1,256]{1,0:T(1,128)S(1)} %bitcast.150), channel_id=1, source_target_pairs={{0,8},{8,16},{16,24},{24,32},{32,40},{40,48},{48,56},{56,64},{64,7... | collective-permute-start | bytes 3080 | tf_op jit(solution)/shard_map/ppermute | solution.py:14
  11.3 312.8 %all-to-all-start = ((f32[8,64,128]{2,1,0:T(8,128)}), f32[8,64,128]{2,1,0:T(8,128)S(1)}, u32[]{:S(2)}, u32[]{:S(2)}) async-start(f32[8,64,128]{2,1,0:T(8,128)} %stack.8), calls=%async_computation | async-start | bytes 524288 | tf_op jit(solution)/shard_map/all_to_all | solution.py:86
  18.4 441.2 %reduce-scatter.5.cloned.1.call-start = ((), (), s32[]{:S(2)}) async-start(), calls=%async_computation.8 | async-start | bytes 294912 | tf_op jit(solution)/shard_map/reduce_scatter | solution.py:149
  18.5 0.7 copy-start.10
  18.5 0.7 copy-start.9
  18.5 0.7 copy-start.5
  163.8 0.7 copy-start.8
  296.4 11.8 copy-start.1
  296.4 11.8 copy-start.3
  309.3 0.7 copy-start.13
  310.0 0.7 copy-start.11
  322.4 0.7 copy-start.12
  328.0 126.1 %copy-start.7 = (f32[256]{0:T(256)S(1)}, f32[256]{0:T(256)}, u32[]{:S(2)}) copy-start(f32[256]{0:T(256)} %param.26) | copy-start | bytes 3076
  456.0 0.7 copy-start.4
  459.6 1.1 copy-start.2
  463.5 112.3 %collective-permute-start.1 = (f32[1,256]{1,0:T(1,128)S(1)}, f32[1,256]{1,0:T(1,128)S(1)}, u32[]{:S(2)}, u32[]{:S(2)}) collective-permute-start(f32[1,256]{1,0:T(1,128)S(1)} %slice.79), channel_id=1, source_target_pairs={{0,504},{8,0},{16,8},{24,16},{32,24},{40,32},{48,40},{56,48},{64,5... | collective-permute-start | bytes 3080 | tf_op jit(solution)/shard_map/ppermute | solution.py:14
  569.4 142.9 %all-to-all-start.1 = ((f32[8,64,128]{2,1,0:T(8,128)}), f32[8,64,128]{2,1,0:T(8,128)S(1)}, u32[]{:S(2)}, u32[]{:S(2)}) async-start(f32[8,64,128]{2,1,0:T(8,128)} %stack.9), calls=%async_computation.2 | async-start | bytes 524288 | tf_op jit(solution)/shard_map/all_to_all | solution.py:86
  574.9 291.6 %reduce-scatter.7.cloned.1.call-start = ((), (), s32[]{:S(2)}) async-start(), calls=%async_computation.9 | async-start | bytes 294912 | tf_op jit(solution)/shard_map/reduce_scatter | solution.py:149
  575.7 0.7 copy-start.6
  728.3 135.3 %collective-permute-start.2 = (f32[1,256]{1,0:T(1,128)S(1)}, f32[1,256]{1,0:T(1,128)S(1)}, u32[]{:S(2)}, u32[]{:S(2)}) collective-permute-start(f32[1,256]{1,0:T(1,128)S(1)} %slice.80), channel_id=1, source_target_pairs={{0,8},{8,16},{16,24},{24,32},{32,40},{40,48},{48,56},{56,64},{64,7... | collective-permute-start | bytes 3080 | tf_op jit(solution)/shard_map/ppermute | solution.py:14
  870.3 112.5 %collective-permute-start.3 = (f32[1,256]{1,0:T(1,128)S(1)}, f32[1,256]{1,0:T(1,128)S(1)}, u32[]{:S(2)}, u32[]{:S(2)}) collective-permute-start(f32[1,256]{1,0:T(1,128)S(1)} %slice.83), channel_id=1, source_target_pairs={{0,504},{8,0},{16,8},{24,16},{32,24},{40,32},{48,40},{56,48},{64,5... | collective-permute-start | bytes 3080 | tf_op jit(solution)/shard_map/ppermute | solution.py:14
  976.3 144.3 %all-to-all-start.2 = ((f32[8,64,128]{2,1,0:T(8,128)}), f32[8,64,128]{2,1,0:T(8,128)S(1)}, u32[]{:S(2)}, u32[]{:S(2)}) async-start(f32[8,64,128]{2,1,0:T(8,128)} %stack.10), calls=%async_computation.4 | async-start | bytes 524288 | tf_op jit(solution)/shard_map/all_to_all | solution.py:86
  981.7 291.3 %reduce-scatter.9.cloned.1.call-start = ((), (), s32[]{:S(2)}) async-start(), calls=%async_computation.10 | async-start | bytes 294912 | tf_op jit(solution)/shard_map/reduce_scatter | solution.py:149
  1117.6 152.5 %collective-permute-start.4 = (f32[1,256]{1,0:T(1,128)S(1)}, f32[1,256]{1,0:T(1,128)S(1)}, u32[]{:S(2)}, u32[]{:S(2)}) collective-permute-start(f32[1,256]{1,0:T(1,128)S(1)} %slice.84), channel_id=1, source_target_pairs={{0,8},{8,16},{16,24},{24,32},{32,40},{40,48},{48,56},{56,64},{64,7... | collective-permute-start | bytes 3080 | tf_op jit(solution)/shard_map/ppermute | solution.py:14
  1276.8 126.0 %collective-permute-start.5 = (f32[1,256]{1,0:T(1,128)S(1)}, f32[1,256]{1,0:T(1,128)S(1)}, u32[]{:S(2)}, u32[]{:S(2)}) collective-permute-start(f32[1,256]{1,0:T(1,128)S(1)} %slice.87), channel_id=1, source_target_pairs={{0,504},{8,0},{16,8},{24,16},{32,24},{40,32},{48,40},{56,48},{64,5... | collective-permute-start | bytes 3080 | tf_op jit(solution)/shard_map/ppermute | solution.py:14
  1382.7 17.3 %all-to-all-start.3 = ((f32[8,64,128]{2,1,0:T(8,128)}), f32[8,64,128]{2,1,0:T(8,128)S(1)}, u32[]{:S(2)}, u32[]{:S(2)}) async-start(f32[8,64,128]{2,1,0:T(8,128)} %stack.11), calls=%async_computation.6 | async-start | bytes 524288 | tf_op jit(solution)/shard_map/all_to_all | solution.py:86
  1388.1 45.6 %reduce-scatter.11.cloned.1.call-start = ((), (), s32[]{:S(2)}) async-start(), calls=%async_computation.11 | async-start | bytes 294912 | tf_op jit(solution)/shard_map/reduce_scatter | solution.py:149
Sparse Core Ops, SparseCore 0:
  327.2 40.4 reduce-scatter.4
  715.4 40.4 reduce-scatter.6
  1123.7 42.6 reduce-scatter.8
  1402.4 31.2 reduce-scatter.10
